TPU v7x, 32 devices: a whole 2x2x4 slice. The times are simulated.
32 devices in a mesh: dp: 8 (over z, core), tensor: 4 (over y, x).
Axes of the slice: x: 2, y: 2, z: 4, core: 2. Of those that a mesh axis runs over, the one named last changes fastest.
Arguments:
- tokens_in: bfloat16 [8192, 1024], P('dp'), may hold values from -6 to 6
- norm_params: float32 [4, 1024], replicated, may hold values from -1.2 to 3.6
- query_key_value_weight: bfloat16 [3, 1024, 1024], P(None, None, 'tensor'), may hold values from -0.09375 to 0.09375
- out_weight: bfloat16 [1024, 1024], P('tensor'), may hold values from -1.5 to 1.5
- fc_weight: bfloat16 [1024, 4096], P(None, 'tensor'), may hold values from -0.1875 to 0.1875
- proj_weight: bfloat16 [4096, 1024], P('tensor'), may hold values from -0.09375 to 0.09375
- factors: float32 [4, 4, 1024], replicated, may hold values from -0.12 to 0.12
- first_moment: float32 [4, 4, 1024], replicated, may hold values from -0.375 to 0.375
- second_moment: float32 [4, 4, 1024], replicated, may hold values from 0.015625 to 0.0625
- grad_out: bfloat16 [8192, 1024], P('dp'), may hold values from -6 to 6
Outputs:
- block_out: bfloat16 [8192, 1024], P(('dp', 'tensor'))
- input_grad: float32 [8192, 1024], P(('dp', 'tensor'))
- clipped_grad: float32 [4, 4, 1024], replicated
- grad_norm: float32 [], replicated
- factors_new: float32 [4, 4, 1024], replicated
- first_new: float32 [4, 4, 1024], replicated
- second_new: float32 [4, 4, 1024], replicated
All inputs are finite; a program needn't handle non-finite values.
Results may differ from a plain program's by a relative error of at most 0.015.
Values may be sent and summed in bfloat16 or wider, within the bound.
A program may use at most 128 MiB of HBM per device.

v0:
```python
import functools

import jax
import jax.numpy as jnp
from jax import lax
from jax.experimental import pallas as pl
from jax.experimental.pallas import tpu as pltpu
from jax.sharding import PartitionSpec as P

HD = 64
SEQ = 1024
STEP = 5


EPSILON = 1e-05
ADAPTER_SCALING = 8.0
CLIP_NORM = 16.0
LEARN_RATE = 0.03
BETA_ONE = 0.5
BETA_TWO = 0.5
WEIGHT_DECAY = 0.01
ADAM_EPSILON = 1e-08
NEG_LARGE = -1e30
GELU_SCALE = 0.7978845608028654
GELU_CUBE = 0.044715


def matrix_product(left, right):
    return jnp.dot(left, right, preferred_element_type=jnp.float32)


def product_with_transpose(left, right):
    return lax.dot_general(
        left, right, (((1,), (1,)), ((), ())), preferred_element_type=jnp.float32
    )


def transpose_then_product(left, right):
    return lax.dot_general(
        left, right, (((0,), (0,)), ((), ())), preferred_element_type=jnp.float32
    )


def normalize(value_rows_local, gain_vec, bias_vec):
    centered = value_rows_local - jnp.mean(value_rows_local, -1, keepdims=True)
    inverse = lax.rsqrt(jnp.mean(centered * centered, -1, keepdims=True) + EPSILON)
    unit_rows = centered * inverse
    return (unit_rows * gain_vec + bias_vec, unit_rows, inverse)


def normalize_back(incoming, unit_rows, inverse, gain_vec):
    scaled = incoming * gain_vec
    return inverse * (
        scaled
        - jnp.mean(scaled, -1, keepdims=True)
        - unit_rows * jnp.mean(scaled * unit_rows, -1, keepdims=True)
    )


def causal_scores(query_block, key_all, block_index, block_len):
    scores = (
        jnp.einsum("bqhd,bkhd->bhqk", query_block, key_all, preferred_element_type=jnp.float32)
        * 0.125
    )
    query_pos = block_index * block_len + jnp.arange(block_len)
    allowed = jnp.arange(SEQ)[None, :] <= query_pos[:, None]
    return jnp.where(allowed, scores, NEG_LARGE)


def attention_forward(query_rows_local, key_all, value_all):
    block_len = min(512, SEQ)
    outputs = []
    logsums = []
    for block_index in range(SEQ // block_len):
        query_block = query_rows_local[:, block_index * block_len : (block_index + 1) * block_len]
        scores = causal_scores(query_block, key_all, block_index, block_len)
        row_max = jnp.max(scores, -1, keepdims=True)
        exponent = jnp.exp(scores - row_max)
        row_total = jnp.sum(exponent, -1, keepdims=True)
        probability = (exponent / row_total).astype(jnp.bfloat16)
        mixture = jnp.einsum(
            "bhqk,bkhd->bqhd", probability, value_all, preferred_element_type=jnp.float32
        )
        outputs.append(mixture.astype(jnp.bfloat16))
        logsums.append(row_max[..., 0] + jnp.log(row_total[..., 0]))
    return (jnp.concatenate(outputs, 1), jnp.concatenate(logsums, 2))


def attention_backward(query_rows_local, key_all, value_all, grad_mixture, logsums):
    block_len = min(512, SEQ)
    grad_queries = []
    grad_keys = jnp.zeros(key_all.shape, jnp.float32)
    value_gradient_rows = jnp.zeros(value_all.shape, jnp.float32)
    for block_index in range(SEQ // block_len):
        lower = block_index * block_len
        query_block = query_rows_local[:, lower : lower + block_len]
        grad_block = grad_mixture[:, lower : lower + block_len]
        scores = causal_scores(query_block, key_all, block_index, block_len)
        probability = jnp.exp(scores - logsums[:, :, lower : lower + block_len, None])
        grad_prob = jnp.einsum(
            "bqhd,bkhd->bhqk", grad_block, value_all, preferred_element_type=jnp.float32
        )
        row_delta = jnp.sum(grad_prob * probability, -1, keepdims=True)
        dscore = (0.125 * (probability * (grad_prob - row_delta))).astype(jnp.bfloat16)
        grad_queries.append(
            jnp.einsum(
                "bhqk,bkhd->bqhd", dscore, key_all, preferred_element_type=jnp.float32
            ).astype(jnp.bfloat16)
        )
        grad_keys = grad_keys + jnp.einsum(
            "bhqk,bqhd->bkhd", dscore, query_block, preferred_element_type=jnp.float32
        )
        value_gradient_rows = value_gradient_rows + jnp.einsum(
            "bhqk,bqhd->bkhd",
            probability.astype(jnp.bfloat16),
            grad_block,
            preferred_element_type=jnp.float32,
        )
    return (
        jnp.concatenate(grad_queries, 1),
        grad_keys.astype(jnp.bfloat16),
        value_gradient_rows.astype(jnp.bfloat16),
    )


def adam_step(factor_grad, weights, first_old, second_old, grad_norm):
    clipped = factor_grad * (CLIP_NORM / jnp.maximum(grad_norm, CLIP_NORM))
    first_new = BETA_ONE * first_old + (1.0 - BETA_ONE) * clipped
    second_new = BETA_TWO * second_old + (1.0 - BETA_TWO) * clipped * clipped
    first_hat = first_new / (1.0 - BETA_ONE**STEP)
    second_hat = second_new / (1.0 - BETA_TWO**STEP)
    weights_new = weights - LEARN_RATE * (
        first_hat / (jnp.sqrt(second_hat) + ADAM_EPSILON) + WEIGHT_DECAY * weights
    )
    return (clipped, weights_new, first_new, second_new)


def body(
    tokens_in,
    norm_params,
    query_key_value_weight,
    out_weight,
    fc_weight,
    proj_weight,
    factors,
    first_moment,
    second_moment,
    grad_out,
):
    tensor_size = lax.axis_size("tensor")
    tensor_rank = lax.axis_index("tensor")
    token_count = tokens_in.shape[0]
    doc_count = token_count // SEQ
    local_width = query_key_value_weight.shape[2]
    heads_here = local_width // HD
    row_count = token_count // tensor_size
    row_start = tensor_rank * row_count
    rank_count = factors.shape[1]
    full_width = factors.shape[2]
    inputs = tokens_in.astype(jnp.float32)
    first_normalized, unit_one, inverse_one = normalize(inputs, norm_params[0], norm_params[1])
    first_normalized_reduced = first_normalized.astype(jnp.bfloat16)
    factor_reduced_precision = factors.astype(jnp.bfloat16)
    column_offset = tensor_rank * local_width
    query_adapter_output = lax.dynamic_slice_in_dim(
        factor_reduced_precision[1], column_offset, local_width, 1
    )
    value_adapter_output = lax.dynamic_slice_in_dim(
        factor_reduced_precision[3], column_offset, local_width, 1
    )
    query_down_factor = product_with_transpose(
        first_normalized_reduced, factor_reduced_precision[0]
    ).astype(jnp.bfloat16)
    value_down_factor = product_with_transpose(
        first_normalized_reduced, factor_reduced_precision[2]
    ).astype(jnp.bfloat16)
    query_rows_local = (
        matrix_product(first_normalized_reduced, query_key_value_weight[0])
        + ADAPTER_SCALING * matrix_product(query_down_factor, query_adapter_output)
    ).astype(jnp.bfloat16)
    keys_low = matrix_product(first_normalized_reduced, query_key_value_weight[1]).astype(
        jnp.bfloat16
    )
    values_low = (
        matrix_product(first_normalized_reduced, query_key_value_weight[2])
        + ADAPTER_SCALING * matrix_product(value_down_factor, value_adapter_output)
    ).astype(jnp.bfloat16)
    head_shape = (doc_count, SEQ, heads_here, HD)
    query_heads = query_rows_local.reshape(head_shape)
    keys_heads = keys_low.reshape(head_shape)
    values_heads = values_low.reshape(head_shape)
    mixture, logsums = attention_forward(query_heads, keys_heads, values_heads)
    attn_part = matrix_product(mixture.reshape(token_count, local_width), out_weight)
    grad_full = grad_out.astype(jnp.float32)
    attn_rows = lax.psum_scatter(
        attn_part.astype(jnp.bfloat16), "tensor", scatter_dimension=0, tiled=True
    ).astype(jnp.float32)
    resid_rows = lax.dynamic_slice_in_dim(inputs, row_start, row_count, 0) + attn_rows
    normed_two_rows, unit_two, inverse_two = normalize(resid_rows, norm_params[2], norm_params[3])
    normed_two_low = lax.all_gather(
        normed_two_rows.astype(jnp.bfloat16), "tensor", axis=0, tiled=True
    )
    hidden_pre = matrix_product(normed_two_low, fc_weight)
    hidden_act, gelu_pull = jax.vjp(
        lambda argument: jax.nn.gelu(argument, approximate=True), hidden_pre
    )
    mlp_part = matrix_product(hidden_act.astype(jnp.bfloat16), proj_weight)
    grad_hidden = product_with_transpose(grad_out, proj_weight)
    grad_pre = gelu_pull(grad_hidden)[0].astype(jnp.bfloat16)
    second_part = product_with_transpose(grad_pre, fc_weight)
    out_rows = resid_rows + lax.psum_scatter(
        mlp_part.astype(jnp.bfloat16), "tensor", scatter_dimension=0, tiled=True
    ).astype(jnp.float32)
    second_rows = lax.psum_scatter(
        second_part.astype(jnp.bfloat16), "tensor", scatter_dimension=0, tiled=True
    ).astype(jnp.float32)
    resid_grad_rows = lax.dynamic_slice_in_dim(grad_full, row_start, row_count, 0) + normalize_back(
        second_rows, unit_two, inverse_two, norm_params[2]
    )
    resid_grad_low = lax.all_gather(
        resid_grad_rows.astype(jnp.bfloat16), "tensor", axis=0, tiled=True
    )
    grad_mixture = product_with_transpose(resid_grad_low, out_weight).astype(jnp.bfloat16)
    query_gradient, grad_keys, value_gradient_rows = attention_backward(
        query_heads, keys_heads, values_heads, grad_mixture.reshape(head_shape), logsums
    )
    query_gradient = query_gradient.reshape(token_count, local_width)
    grad_keys = grad_keys.reshape(token_count, local_width)
    value_gradient_rows = value_gradient_rows.reshape(token_count, local_width)
    stacked = jnp.stack((query_gradient, grad_keys, value_gradient_rows))
    first_part = jnp.einsum(
        "stc,sdc->td", stacked, query_key_value_weight, preferred_element_type=jnp.float32
    )
    query_up_factor = ADAPTER_SCALING * product_with_transpose(query_gradient, query_adapter_output)
    value_up_factor = ADAPTER_SCALING * product_with_transpose(
        value_gradient_rows, value_adapter_output
    )
    first_part = first_part + jnp.dot(
        query_up_factor,
        factor_reduced_precision[0].astype(jnp.float32),
        precision=lax.Precision.HIGHEST,
    )
    first_part = first_part + jnp.dot(
        value_up_factor,
        factor_reduced_precision[2].astype(jnp.float32),
        precision=lax.Precision.HIGHEST,
    )
    first_rows = lax.psum_scatter(
        first_part.astype(jnp.bfloat16), "tensor", scatter_dimension=0, tiled=True
    ).astype(jnp.float32)
    unit_rows = lax.dynamic_slice_in_dim(unit_one, row_start, row_count, 0)
    inverse_rows = lax.dynamic_slice_in_dim(inverse_one, row_start, row_count, 0)
    input_rows = resid_grad_rows + normalize_back(
        first_rows, unit_rows, inverse_rows, norm_params[0]
    )
    query_cross_term = transpose_then_product(query_gradient, first_normalized_reduced)
    value_cross_term = transpose_then_product(value_gradient_rows, first_normalized_reduced)
    query_down_gradient = ADAPTER_SCALING * jnp.dot(
        query_adapter_output.astype(jnp.float32), query_cross_term, precision=lax.Precision.HIGHEST
    )
    value_down_gradient = ADAPTER_SCALING * jnp.dot(
        value_adapter_output.astype(jnp.float32), value_cross_term, precision=lax.Precision.HIGHEST
    )
    empty_slot = jnp.zeros((rank_count, full_width), jnp.float32)
    up_grad_query = lax.dynamic_update_slice_in_dim(
        empty_slot,
        ADAPTER_SCALING * transpose_then_product(query_down_factor, query_gradient),
        column_offset,
        1,
    )
    up_grad_value = lax.dynamic_update_slice_in_dim(
        empty_slot,
        ADAPTER_SCALING * transpose_then_product(value_down_factor, value_gradient_rows),
        column_offset,
        1,
    )
    partial_grad = jnp.stack(
        (query_down_gradient, up_grad_query, value_down_gradient, up_grad_value)
    )
    reduced = lax.psum(partial_grad, ("dp", "tensor"))
    grad_norm = jnp.sqrt(jnp.sum(reduced * reduced))
    clipped, weights_new, first_new, second_new = adam_step(
        reduced, factors, first_moment, second_moment, grad_norm
    )
    return (
        out_rows.astype(jnp.bfloat16),
        input_rows,
        clipped,
        grad_norm,
        weights_new,
        first_new,
        second_new,
    )


MESH = pl.DeviceIdType.MESH
BF = jnp.bfloat16
F32 = jnp.float32
GROUPS = 8
PAIRS = 8


def mm(left, right):
    return jnp.dot(left, right, preferred_element_type=F32)


def mm_nt(left, right):
    return lax.dot_general(left, right, (((1,), (1,)), ((), ())), preferred_element_type=F32)


def mm_tn(left, right):
    return lax.dot_general(left, right, (((0,), (0,)), ((), ())), preferred_element_type=F32)


def flip(value, bit):
    return value + bit - 2 * bit * ((value // bit) % 2)


def unit_of(rows):
    centered = rows - jnp.mean(rows, -1, keepdims=True)
    inverse = lax.rsqrt(jnp.mean(centered * centered, -1, keepdims=True) + EPSILON)
    return centered * inverse, inverse


def unit_back(scaled, unit, inverse):
    return inverse * (
        scaled - jnp.mean(scaled, -1, keepdims=True) - unit * jnp.mean(scaled * unit, -1, keepdims=True)
    )


def fused_kernel(
    planes,
    tokens, norm_params, wqkv, w_out, w_fc, w_proj, factors, grad_out,
    bo_r, ig_r, summed,
    tok, n1, go, wq, wkv, wo, fcw, pw, kv, qs, p0, p1, mix, inv, attn_own, attn_s, attn_r,
    res, n2, acc_a, acc_b, gnt_s, gnt_r, gnt_xs, gnt_xr, mlp_s, mlp_r, mlp_xs, mlp_xr,
    gr, gr_b, bo_f, bo_s, gq, dos, gno_s, gno_r, gno_xs, gno_xr, ig_s,
    fpad, f02, f1p, f3kv, down, gd_scr, fg_a, fg_q, fg_v, ps, ps_r, plane_buf, z_buf, fin,
    chain_send, chain_recv, pair_send, pair_recv, load_sem, ssem, rsem,
):
    d = lax.axis_index("dp")
    t = lax.axis_index("tensor")
    z, c, x, y = d // 2, d % 2, t % 2, t // 2
    odd = z % 2
    nbr = (flip(d, 1), t)
    prim = (d, flip(t, 1 + odd))
    sec = (d, flip(t, 2 - odd))
    plane = [(d, flip(t, 1)), (d, flip(t, 2)), (d, 3 - t)]
    x_nbr, y_nbr = plane[0], plane[1]
    zs = [(flip(d, 2 << k), t) for k in range(planes.bit_length() - 1)]
    owners = [(2 * z + y, 2 * h + x) for h in range(2)]
    at_home = [jnp.logical_and(c == y, h == y) for h in range(2)]
    quarter = [t, flip(t, 1 + odd), flip(t, 2 - odd), 3 - t]
    column = [pl.multiple_of(q * 256 + c * 128, 128) for q in quarter]

    def at(start, size):
        return pl.ds(pl.multiple_of(start, size), size)

    def rows_of(half, side):
        return at(512 * half + 256 * side, 256)

    def own_rows(h, side):
        return at(512 * h + 256 * side + 128 * c, 128)

    def other_rows(h, side):
        return at(512 * h + 256 * side + 128 * (1 - c), 128)

    def remote_to(src, dst, out_index, in_index, device):
        return pltpu.make_async_remote_copy(
            src_ref=src, dst_ref=dst, send_sem=ssem.at[out_index], recv_sem=rsem.at[in_index],
            device_id=device, device_id_type=MESH,
        )

    def remote(src, dst, index, device):
        return remote_to(src, dst, index, index, device)

    pending = []

    def drain():
        for wait in pending:
            wait()

    def send(copy):
        copy.start()
        pending.append(copy.wait_send)
        return copy

    lane = at(c * 128, 128)
    loads = [
        pltpu.make_async_copy(wqkv.at[1, :, lane], wkv.at[:, pl.ds(0, 128)], load_sem.at[0]),
        pltpu.make_async_copy(wqkv.at[2, :, lane], wkv.at[:, pl.ds(128, 128)], load_sem.at[1]),
        pltpu.make_async_copy(wqkv.at[0, :, lane], wq.at[:, pl.ds(0, 128)], load_sem.at[2]),
        pltpu.make_async_copy(w_out.at[lane, :], wo.at[pl.ds(0, 128), :], load_sem.at[3]),
        pltpu.make_async_copy(w_fc.at[:, at(c * 512, 512)], fcw.at[0], load_sem.at[4]),
        pltpu.make_async_copy(w_proj.at[at(c * 512, 512), :], pw.at[0], load_sem.at[5]),
    ]
    for load in loads:
        load.start()

    barrier = pltpu.get_barrier_semaphore()
    partners = [nbr, x_nbr, y_nbr] + zs
    for device in partners:
        pl.semaphore_signal(barrier, inc=1, device_id=device, device_id_type=MESH)
    pl.semaphore_wait(barrier, len(partners))

    doc = []
    for first, source, target in ((0, tokens, tok), (4, grad_out, go)):
        for r in range(4):
            part = pl.ds(256 * r, 256)
            doc.append((source.at[part, :], target.at[part, :], first + r))

    @pl.when(c == y)
    def _():
        for src, dst, index in doc:
            remote(src, dst, index, nbr).start()
            pltpu.make_async_copy(src, dst, rsem.at[index]).start()

    def doc_sent():
        @pl.when(c == y)
        def _():
            for item in doc:
                remote(*item, nbr).wait_send()

    pending.append(doc_sent)

    def doc_wait(index):
        remote(*doc[index], nbr).wait_recv()

    def piece(slot, group):
        matrix, a = group // 2, group % 2
        if matrix < 2:
            return wkv.at[pl.ds(512 * a, 512), pl.ds(256 * slot + 128 * matrix, 128)]
        if matrix == 2:
            return wq.at[pl.ds(512 * a, 512), pl.ds(128 * slot, 128)]
        return wo.at[pl.ds(128 * slot + 64 * a, 64), :]

    def hop(slot, group):
        return pltpu.make_async_remote_copy(
            src_ref=piece(1 if slot > 1 else 0, group), dst_ref=piece(slot, group),
            send_sem=chain_send.at[slot - 1, group], recv_sem=chain_recv.at[slot - 1, group],
            device_id=(prim, zs[0], sec)[slot - 1], device_id_type=MESH,
        )

    def pump(group, later=True):
        hop(1, group).wait_recv()
        for slot in (2, 3):
            hop(slot, group).start()
            if later:
                pending.append(hop(slot, group).wait_send)

    def passed(groups):
        for group in groups:
            hop(2, group).wait_recv()
            hop(3, group).wait_recv()

    def pair_piece(slot, pair, parity):
        h, q = pair // 4, pair % 4
        if q < 2:
            return fcw.at[slot, at(512 * q + 256 * parity, 256), pl.ds(256 * h, 256)]
        return pw.at[slot, at(256 * h + 128 * (q - 2) + 64 * parity, 64), :]

    def pair_hop(step, pair, parity):
        return pltpu.make_async_remote_copy(
            src_ref=pair_piece(step, pair, parity), dst_ref=pair_piece(1, pair, parity),
            send_sem=pair_send.at[step, pair], recv_sem=pair_recv.at[step, pair],
            device_id=(y_nbr, zs[0])[step], device_id_type=MESH,
        )

    def pair_pump(pair):
        pair_hop(0, pair, odd).wait_recv()
        pair_hop(1, pair, odd).start()

    def pair_wait(pairs):
        for pair in pairs:
            pair_hop(1, pair, 1 - odd).wait_recv()

    for matrix in range(4):
        loads[matrix].wait()
        send(hop(1, 2 * matrix))
        send(hop(1, 2 * matrix + 1))

    fpad[...] = jnp.zeros_like(fpad)
    fpad[0:4, :] = factors[0]
    fpad[4:8, :] = factors[2]
    f02[...] = fpad[...].astype(BF)
    fpad[...] = jnp.zeros_like(fpad)
    for s in range(4):
        fpad[0:4, 128 * s : 128 * s + 128] = factors[1, :, pl.ds(column[s], 128)]
    f1p[...] = fpad[:, :512].astype(BF)
    fpad[...] = jnp.zeros_like(fpad)
    for s in range(4):
        fpad[4:8, 256 * s + 128 : 256 * s + 256] = factors[3, :, pl.ds(column[s], 128)]
    f3kv[...] = fpad[...].astype(BF)
    ps[...] = jnp.zeros_like(ps)

    gain_one, bias_one = norm_params[0:1, :], norm_params[1:2, :]
    gain_two, bias_two = norm_params[2:3, :], norm_params[3:4, :]
    def first_norm(r):
        doc_wait(r)

        @pl.loop(0, 2)
        def _(q):
            rows = at(256 * r + 128 * q, 128)
            unit, _ = unit_of(tok[rows, :].astype(F32))
            n1[rows, :] = (unit * gain_one + bias_one).astype(BF)

    first_norm(0)
    first_norm(1)
    pump(0)
    first_norm(2)
    first_norm(3)

    @pl.loop(0, 2)
    def _(r):
        rows = at(512 * r, 512)
        down[rows, :] = mm_nt(n1[rows, :], f02[...]).astype(BF)

    pump(1)
    acc_a[...] = jnp.zeros_like(acc_a)
    acc_b[...] = jnp.zeros_like(acc_b)
    first_head = lax.broadcasted_iota(jnp.int32, (256, 512), 1) % 128 < 64
    first_lanes = first_head[:, 0:128]

    def stacked(rows, lanes):
        return jnp.concatenate((jnp.where(lanes, rows, 0.0), jnp.where(lanes, 0.0, rows)), 0)

    p_refs = (p0, p1)
    column_pos = lax.broadcasted_iota(jnp.int32, (512, 512), 1)
    row_pos = lax.broadcasted_iota(jnp.int32, (512, 512), 0) % 256 + 256 * x
    allowed = column_pos <= row_pos

    loads[4].wait()
    loads[5].wait()

    @pl.loop(0, 4)
    def _(s):
        @pl.when(s == 1)
        def _():
            for group in range(2, 6):
                pump(group, False)

        @pl.when(s == 2)
        def _():
            pump(6, False)
            passed(range(0, 6))

        @pl.when(s == 3)
        def _():
            pump(7, False)
            for pair in range(PAIRS):
                pair_hop(0, pair, odd).start()

        both_lanes, lanes = at(256 * s, 256), at(128 * s, 128)
        keys, values = at(256 * s, 128), at(256 * s + 128, 128)

        @pl.loop(0, 2)
        def _(r):
            rows = at(512 * r, 512)
            kv[rows, both_lanes] = (
                mm(n1[rows, :], wkv[:, both_lanes]) + ADAPTER_SCALING * mm(down[rows, :], f3kv[:, both_lanes])
            ).astype(BF)

        for h in range(2):
            rows = rows_of(h, x)
            query = mm(n1[rows, :], wq[:, lanes]) + ADAPTER_SCALING * mm(down[rows, :], f1p[:, lanes])
            qs[h, :, lanes] = stacked(query.astype(BF).astype(F32) * 0.125, first_lanes).astype(BF)
        scores = [mm_nt(qs[h, :, lanes], kv[0 : 512 * (h + 1), keys]) for h in range(2)]
        kept = []
        for h in range(2):
            last = jnp.where(allowed, scores[h][:, 512 * h :], NEG_LARGE)
            block = jnp.concatenate((scores[h][:, :512], last), 1) if h else last
            exponent = jnp.exp(block - jnp.max(block, -1, keepdims=True))
            inverse = 1.0 / jnp.sum(exponent, -1, keepdims=True)
            p_refs[h][s] = exponent.astype(BF)
            inv[h, :, lanes] = jnp.broadcast_to(inverse, (512, 128))
            kept.append((exponent.astype(BF), inverse))
        for h in range(2):
            both = mm(kept[h][0], kv[0 : 512 * (h + 1), values]) * kept[h][1]
            mix[256 * h : 256 * h + 256, lanes] = jnp.where(first_lanes, both[0:256], both[256:512])

    for group in range(2, GROUPS):
        pending.append(hop(2, group).wait_send)
        pending.append(hop(3, group).wait_send)
    for pair in range(PAIRS):
        pending.append(pair_hop(0, pair, odd).wait_send)
    passed(range(6, 8))

    def heads_out(sub):
        rows = [mix[at(256 * h + 128 * sub, 128), :].astype(BF) for h in range(2)]
        return mm(jnp.concatenate(rows, 0), wo[...])

    attn_s[...] = heads_out(1 - c).astype(BF)
    to_nbr = send(remote(attn_s, attn_r, 8, nbr))
    attn_own[...] = heads_out(c)
    to_nbr.wait_recv()

    gathered = []
    for h in range(2):
        part = slice(128 * h, 128 * h + 128)
        rows = own_rows(h, x)
        residual = tok[rows, :].astype(F32) + attn_own[part, :] + attn_r[part, :].astype(F32)
        res[part, :] = residual
        unit, _ = unit_of(residual)
        n2[rows, :] = (unit * gain_two + bias_two).astype(BF)
        gathered.append(send(remote(n2.at[rows, :], n2.at[rows, :], 11 + h, x_nbr)))
        gathered.append(send(remote(n2.at[rows, :], n2.at[rows, :], 9 + h, nbr)))
    for r in range(4):
        doc_wait(4 + r)
    gathered[1].wait_recv()
    gathered[3].wait_recv()

    def pass_on(h):
        gathered[2 * h].wait_recv()
        rows = own_rows(h, 1 - x)
        remote(n2.at[rows, :], n2.at[rows, :], 13 + h, nbr).start()

    def passed_on(h):
        rows = own_rows(h, 1 - x)
        return remote(n2.at[rows, :], n2.at[rows, :], 13 + h, nbr)

    def sum_copy(source, target, first, h, j):
        part = pl.ds(128 * j, 128)
        return remote(source.at[h, part, :], target.at[h, part, :], first + 2 * h + j, nbr)

    def to_core(acc, source, target, first, h):
        for j, side in enumerate((1 - x, x)):
            source[h, 128 * j : 128 * j + 128, :] = acc[other_rows(h, side), :].astype(BF)
            sum_copy(source, target, first, h, j).start()

    def to_side(acc, source, target, out, out_target, first, side_first, h):
        sum_copy(source, target, first, h, 0).wait_recv()
        out[h] = (acc[own_rows(h, 1 - x), :] + target[h, 0:128, :].astype(F32)).astype(BF)
        return send(remote(out.at[h], out_target.at[h], side_first + h, x_nbr))

    @pl.loop(0, 8)
    def _(unit):
        @pl.when(unit == 0)
        def _():
            pair_pump(0)

        @pl.when(unit == 2)
        def _():
            for pair in (1, 2):
                pair_pump(pair)
            pass_on(0)
            for pair in (3, 4):
                pair_pump(pair)
            pair_wait(range(0, 4))

        @pl.when(unit == 3)
        def _():
            pass_on(1)
            pair_pump(5)
            for h in range(2):
                passed_on(h).wait_recv()

        @pl.when(unit == 5)
        def _():
            pair_pump(6)

        @pl.when(unit == 6)
        def _():
            pair_pump(7)
            pair_wait(range(4, 8))

        @pl.when(unit == 7)
        def _():
            to_core(acc_b, gnt_s, gnt_r, 40, 1)

        flag = lambda value: jnp.where(value, 1, 0)
        slot = flag(jnp.logical_or(unit == 2, unit >= 5))
        part = flag(jnp.logical_or(unit >= 6, jnp.logical_or(unit == 1, unit == 4)))
        side = jnp.where(unit < 3, x, 1 - x)
        last_half = 7 - unit
        starts = [
            jnp.where(unit < 6, 512 * h + 256 * side, 512 * last_half + 256 * h) for h in range(2)
        ]
        tiles = [at(start, 256) for start in starts]
        lanes = at(256 * part, 256)
        pre = [mm(n2[rows, :], fcw[slot, :, lanes]) for rows in tiles]
        grad_act = [mm_nt(go[rows, :], pw[slot, lanes, :]) for rows in tiles]
        for rows, hidden, grad in zip(tiles, pre, grad_act):
            square = hidden * hidden
            tanh = jnp.tanh(GELU_SCALE * hidden * (1.0 + GELU_CUBE * square))
            half_up = 0.5 * (1.0 + tanh)
            slope = half_up + (0.5 * GELU_SCALE) * hidden * (1.0 - tanh * tanh) * (
                1.0 + 3.0 * GELU_CUBE * square
            )
            acc_b[rows, :] += mm_nt((grad * slope).astype(BF), fcw[slot, :, lanes])
            acc_a[rows, :] += mm((hidden * half_up).astype(BF), pw[slot, lanes, :])

    for pair in range(PAIRS):
        pending.append(pair_hop(1, pair, odd).wait_send)
    for h in range(2):
        pending.append(passed_on(h).wait_send)
        for j in range(2):
            pending.append(sum_copy(gnt_s, gnt_r, 40, h, j).wait_send)
            pending.append(sum_copy(mlp_s, mlp_r, 44, h, j).wait_send)

    gnt_side, mlp_side = [None, None], [None, None]
    to_core(acc_b, gnt_s, gnt_r, 40, 0)
    for h in (1, 0):
        gnt_side[h] = to_side(acc_b, gnt_s, gnt_r, gnt_xs, gnt_xr, 40, 17, h)
    for h in (1, 0):
        to_core(acc_a, mlp_s, mlp_r, 44, h)
    for h in (1, 0):
        mlp_side[h] = to_side(acc_a, mlp_s, mlp_r, mlp_xs, mlp_xr, 44, 21, h)
    for h in range(2):
        part = slice(128 * h, 128 * h + 128)
        sum_copy(mlp_s, mlp_r, 44, h, 1).wait_recv()
        bo_f[part, :] = res[part, :] + acc_a[own_rows(h, x), :] + mlp_r[h, 128:256, :].astype(F32)

    def residual_back(h):
        part = slice(128 * h, 128 * h + 128)
        unit, inverse = unit_of(res[part, :])
        sum_copy(gnt_s, gnt_r, 40, h, 1).wait_recv()
        total = acc_b[own_rows(h, x), :] + gnt_r[h, 128:256, :].astype(F32)
        gnt_side[h].wait_recv()
        scaled = (total + gnt_xr[h].astype(F32)) * gain_two
        grad = go[own_rows(h, x), :].astype(F32) + unit_back(scaled, unit, inverse)
        gr[part, :] = grad
        local = at(256 * h + 128 * c, 128)
        gr_b[local, :] = grad.astype(BF)
        return send(remote(gr_b.at[local, :], gr_b.at[local, :], 23 + h, nbr))

    def mixture_back(h):
        grad_mixture = mm_nt(gr_b[256 * h : 256 * h + 256, :], wo[...])
        dos[h] = (stacked(grad_mixture, first_head) * inv[h]).astype(BF)

    to_nbr = residual_back(1)
    to_nbr.wait_recv()
    mixture_back(1)

    def scores_back(h, first, count):
        size = 512 * (h + 1)
        group = [first + k for k in range(count)]
        lanes = [at(128 * s, 128) for s in group]
        k_lanes = [at(256 * s, 128) for s in group]
        v_lanes = [at(256 * s + 128, 128) for s in group]
        grads = [dos[h, :, lane] for lane in lanes]
        grad_prob = [mm_nt(grad, kv[0:size, lane]) for lane, grad in zip(v_lanes, grads)]
        dscores = []
        for s, lane, grad, block in zip(group, lanes, grads, grad_prob):
            mixture = mix[256 * h : 256 * h + 256, lane]
            delta = jnp.sum(
                grad.astype(F32) * jnp.concatenate((mixture, mixture), 0), -1, keepdims=True
            )
            dscores.append((p_refs[h][s].astype(F32) * (block - delta)).astype(BF))
        for k, (s, lane, grad, dscore) in enumerate(zip(group, lanes, grads, dscores)):
            both = 0.125 * mm(dscore, kv[0:size, k_lanes[k]])
            gq[:, lane] = jnp.where(first_lanes, both[0:256], both[256:512]).astype(BF)
            grad_keys = mm_tn(dscore, qs[h, :, lane])
            grad_values = mm_tn(p_refs[h][s], grad)
            if h:
                acc_a[:, k_lanes[k]] = grad_keys
                acc_a[:, v_lanes[k]] = grad_values
            else:
                acc_a[0:512, k_lanes[k]] += grad_keys
                acc_a[0:512, v_lanes[k]] += grad_values

    def factors_back(h):
        rows = slice(512 * h, 512 * h + 512)
        grads = acc_a[rows, :].astype(BF)
        query = gq[...]
        gd_scr[...] = ADAPTER_SCALING * mm_nt(grads, f3kv[...])
        gd_scr[at(256 * x, 256), :] += ADAPTER_SCALING * mm_nt(query, f1p[...])
        terms = (
            mm_tn(gd_scr[...].astype(BF), n1[rows, :])[0:8],
            mm_tn(down[rows_of(h, x), :], query)[0:8],
            mm_tn(down[rows, :], grads)[0:8],
        )
        for total, term in zip((fg_a, fg_q, fg_v), terms):
            total[...] = term if h else total[...] + term

    def rows_copy(h, j):
        part = pl.ds(128 * j, 128)
        return remote(gno_s.at[h, part, :], gno_r.at[h, part, :], 27 + 2 * h + j, nbr)

    def rows_back(h):
        for j, side in enumerate((1 - x, x)):
            rows = rows_of(h, side)
            grad = mm_nt(acc_a[rows, :].astype(BF), wkv[...])
            grad += mm(gd_scr[at(256 * side, 256), :].astype(BF), f02[...])
            if j:
                grad += mm_nt(gq[...], wq[...])
            acc_b[rows, :] = grad
            gno_s[h, 128 * j : 128 * j + 128, :] = acc_b[other_rows(h, side), :].astype(BF)
            send(rows_copy(h, j))

    side_copies = {}

    def reduce_rows(h):
        rows_copy(h, 0).wait_recv()
        gno_xs[h] = (acc_b[own_rows(h, 1 - x), :] + gno_r[h, 0:128, :].astype(F32)).astype(BF)
        for k in range(2):
            part = pl.ds(64 * k, 64)
            side_copies[h, k] = send(
                remote(gno_xs.at[h, part, :], gno_xr.at[h, part, :], 48 + 2 * h + k, x_nbr)
            )

    def to_owner(src, dst, h, out_index, in_index):
        @pl.when(at_home[h])
        def _():
            pltpu.make_async_copy(src, dst, rsem.at[in_index + c]).start()

        @pl.when(jnp.logical_not(at_home[h]))
        def _():
            remote_to(src, dst, out_index, in_index + c, owners[h]).start()

        def sent():
            @pl.when(jnp.logical_not(at_home[h]))
            def _():
                remote_to(src, dst, out_index, in_index + c, owners[h]).wait_send()

        pending.append(sent)

    def input_rows(h, k):
        if k == 0:
            rows_copy(h, 1).wait_recv()
        start = 512 * h + 256 * x + 128 * c + 64 * k
        rows, part = at(start, 64), slice(64 * k, 64 * k + 64)
        unit, inverse = unit_of(tok[rows, :].astype(F32))
        total = acc_b[rows, :] + gno_r[h, 128 + 64 * k : 192 + 64 * k, :].astype(F32)
        side_copies[h, k].wait_recv()
        scaled = (total + gno_xr[h, part, :].astype(F32)) * gain_one
        out = slice(128 * h + 64 * k, 128 * h + 64 * k + 64)
        ig_s[out, :] = (gr[out, :] + unit_back(scaled, unit, inverse)).astype(BF)
        to_owner(ig_s.at[out, :], ig_r.at[at(128 * c + 64 * k, 64), :], h, 52 + 2 * h + k, 56 + 2 * k)

    @pl.loop(0, 2)
    def _(group):
        scores_back(1, 2 * group, 2)

    to_nbr = residual_back(0)
    factors_back(1)
    rows_back(1)
    to_nbr.wait_recv()
    mixture_back(0)
    reduce_rows(1)
    scores_back(0, 0, 4)

    for h in (1, 0):
        part = slice(128 * h, 128 * h + 128)
        mlp_side[h].wait_recv()
        bo_s[part, :] = (bo_f[part, :] + mlp_xr[h].astype(F32)).astype(BF)
        to_owner(bo_s.at[part, :], bo_r.at[at(128 * c, 128), :], h, 60 + h, 62)
    factors_back(0)

    ps[0:8, :] = fg_a[...]
    down_rows = lax.broadcasted_iota(jnp.int32, (8, 128), 0) < 4
    for s in range(4):
        ps[8:16, pl.ds(column[s], 128)] = ADAPTER_SCALING * jnp.where(
            down_rows, fg_q[:, 128 * s : 128 * s + 128], fg_v[:, 256 * s + 128 : 256 * s + 256]
        )
    core_sum = send(remote(ps, ps_r, 33, nbr))
    rows_back(0)
    core_sum.wait_recv()
    eight = at(8 * c, 8)
    plane_buf[t] = ps[eight, :] + ps_r[eight, :]
    copies = [
        send(remote(plane_buf.at[t], plane_buf.at[t], 35 + k, device)) for k, device in enumerate(plane)
    ]
    reduce_rows(0)
    for k in range(2):
        input_rows(1, k)
    for copy in copies:
        copy.wait_recv()
    z_buf[0] = plane_buf[0] + plane_buf[1] + plane_buf[2] + plane_buf[3]

    def z_copy(k):
        return remote(z_buf.at[2 * k], z_buf.at[2 * k + 1], 64 + k, zs[k])

    for k in range(len(zs)):
        send(z_copy(k))
        if k < 2:
            input_rows(0, k)
        z_copy(k).wait_recv()
        z_buf[2 * k + 2] = z_buf[2 * k] + z_buf[2 * k + 1]
    for k in range(len(zs), 2):
        input_rows(0, k)
    fin[eight, :] = z_buf[2 * len(zs)]
    send(remote(fin.at[eight, :], fin.at[eight, :], 34, nbr))
    theirs = at(8 - 8 * c, 8)
    remote(fin.at[theirs, :], fin.at[theirs, :], 34, nbr).wait_recv()
    result = pltpu.make_async_copy(fin, summed, load_sem.at[0])
    result.start()

    for core in range(2):
        part = pl.ds(128 * core, 128)
        remote_to(bo_s.at[pl.ds(0, 128), :], bo_r.at[part, :], 60, 62 + core, nbr).wait_recv()
        for k in range(2):
            part = pl.ds(128 * core + 64 * k, 64)
            remote_to(ig_s.at[pl.ds(0, 64), :], ig_r.at[part, :], 52, 56 + 2 * k + core, nbr).wait_recv()
    result.wait()
    drain()


def finish_kernel(
    factors, first_moment, second_moment, bo_in, ig_in, sum_in,
    block_out, input_grad, clipped, grad_norm, factors_new, first_new, second_new,
    bo, ig, summed, grads, sem, out_sem,
):
    pairs = [(sum_in, summed), (bo_in, bo), (ig_in, ig)]
    loads = [pltpu.make_async_copy(*pair, sem.at[k]) for k, pair in enumerate(pairs)]
    for load in loads:
        load.start()
    loads[0].wait()
    grad = summed[...]
    norm = jnp.sqrt(jnp.sum(grad * grad, (0, 1), keepdims=True))
    grad_norm[...] = norm
    grad = grad * (CLIP_NORM / jnp.maximum(norm, CLIP_NORM))
    for index, first in enumerate((0, 8, 4, 12)):
        value, weights = grad[first : first + 4], factors[index]
        first_value = BETA_ONE * first_moment[index] + (1.0 - BETA_ONE) * value
        second_value = BETA_TWO * second_moment[index] + (1.0 - BETA_TWO) * value * value
        first_hat = first_value / (1.0 - BETA_ONE**STEP)
        second_hat = second_value / (1.0 - BETA_TWO**STEP)
        clipped[index] = value
        first_new[index] = first_value
        second_new[index] = second_value
        factors_new[index] = weights - LEARN_RATE * (
            first_hat / (jnp.sqrt(second_hat) + ADAM_EPSILON) + WEIGHT_DECAY * weights
        )
    loads[1].wait()
    stores = [pltpu.make_async_copy(bo, block_out, out_sem.at[0])]
    stores[0].start()
    loads[2].wait()
    grads[...] = ig[...].astype(F32)
    stores.append(pltpu.make_async_copy(grads, input_grad, out_sem.at[1]))
    stores[1].start()
    for store in stores:
        store.wait()


def fused(planes, tokens, norm_params, wqkv, w_out, w_fc, w_proj, factors, first, second, grad_out):
    vmem = pl.BlockSpec(memory_space=pltpu.VMEM)
    hbm = pl.BlockSpec(memory_space=pl.ANY)

    def buf(*shape):
        return pltpu.VMEM(shape, BF)

    def acc(*shape):
        return pltpu.VMEM(shape, F32)

    def sems(*shape):
        return pltpu.SemaphoreType.DMA(shape)

    quarter = [buf(256, 1024)] * 2
    halves, eighths = [buf(2, 256, 1024)] * 2, [buf(2, 128, 1024)] * 2
    scratch = [
        buf(1024, 1024), buf(1024, 1024), buf(1024, 1024), buf(1024, 512), buf(1024, 1024), buf(512, 1024),
        buf(2, 1024, 512), buf(2, 512, 1024), buf(1024, 1024), buf(2, 512, 512), buf(4, 512, 512),
        buf(4, 512, 1024), acc(512, 512), acc(2, 512, 512), acc(256, 1024), *quarter,
        acc(256, 1024), buf(1024, 1024), acc(1024, 1024), acc(1024, 1024),
        *halves, *eighths, *halves, *eighths,
        acc(256, 1024), buf(512, 1024), acc(256, 1024), buf(256, 1024), buf(256, 512), buf(2, 512, 512),
        *halves, *eighths, buf(256, 1024),
        acc(128, 1024), buf(128, 1024), buf(128, 512), buf(128, 1024), buf(1024, 128), acc(512, 128),
        acc(8, 1024), acc(8, 512), acc(8, 1024), acc(16, 1024), acc(16, 1024), acc(4, 8, 1024),
        acc(2 * planes, 8, 1024), acc(16, 1024),
        sems(3, GROUPS), sems(3, GROUPS), sems(2, PAIRS), sems(2, PAIRS), sems(6), sems(64 + planes),
        sems(64 + planes),
    ]
    rows = jax.ShapeDtypeStruct((256, 1024), BF)
    passed = pl.pallas_call(
        functools.partial(fused_kernel, planes),
        name="block_step",
        out_shape=(rows, rows, jax.ShapeDtypeStruct((16, 1024), F32)),
        in_specs=[hbm, vmem, hbm, hbm, hbm, hbm, vmem, hbm],
        out_specs=(hbm,) * 3,
        scratch_shapes=scratch,
        compiler_params=pltpu.CompilerParams(
            collective_id=1, has_side_effects=True, vmem_limit_bytes=63 << 20
        ),
    )(tokens, norm_params, wqkv, w_out, w_fc, w_proj, factors, grad_out)
    small = jax.ShapeDtypeStruct((4, 4, 1024), F32)
    outs = pl.pallas_call(
        finish_kernel,
        name="finish_step",
        out_shape=(
            rows, jax.ShapeDtypeStruct((256, 1024), F32), small,
            jax.ShapeDtypeStruct((1, 1), F32), small, small, small,
        ),
        in_specs=[vmem] * 3 + [hbm] * 3,
        out_specs=(hbm, hbm) + (vmem,) * 5,
        scratch_shapes=[*quarter, acc(16, 1024), acc(256, 1024), sems(3), sems(2)],
        compiler_params=pltpu.CompilerParams(vmem_limit_bytes=62 << 20),
    )(factors, first, second, *passed)
    return outs[:3] + (outs[3].reshape(()),) + outs[4:]


def solution(mesh):
    placed = (
        P("dp", None),
        P(),
        P(None, None, "tensor"),
        P("tensor", None),
        P(None, "tensor"),
        P("tensor", None),
        P(),
        P(),
        P(),
        P("dp", None),
    )
    planes = mesh.shape["dp"] // 2

    def step(*args):
        rows, width = args[0].shape
        shapes = (rows, width, args[4].shape[1], args[2].shape[2], args[6].shape[1])
        fits = mesh.shape["tensor"] == 4 and mesh.shape["dp"] % 4 == 0
        if fits and shapes == (SEQ, 1024, 1024, 256, 4):
            return fused(planes, *args)
        return body(*args)

    return jax.shard_map(
        step,
        mesh=mesh,
        in_specs=placed,
        out_specs=(P(("dp", "tensor"), None), P(("dp", "tensor"), None), P(), P(), P(), P(), P()),
        check_vma=False,
    )
```

profile of v0, /device:TPU:1, one launch (start us, length us, event | category | flops | bytes accessed | tf_op | source)
XLA Modules:
  0.0 121.9 jit_solution(9087664298392625675)
XLA Ops:
  0.6 117.2 %block_step.1 = (bf16[256,1024]{1,0:T(8,128)(2,1)}, bf16[256,1024]{1,0:T(8,128)(2,1)}, f32[16,1024]{1,0:T(8,128)}) custom-call(bf16[1024,1024]{1,0:T(8,128)(2,1)} %tokens.1, f32[4,1024]{1,0:T(4,128)} %norm_params.1, bf16[3,1024,256]{2,1,0:T(8,128)(2,1)} %wqkv.1, bf16[256,1024]{1,0:T(8,128)(2,1)} %w_out.1, bf16[1024,1024]{1,0:T(8,128)(2,1)} %w_fc.1, ...), custom_call_target="tpu_custom_call" | custom-call | tf_op jit(solution)/shard_map/block_step/pallas_call | solution.py:965
  117.8 3.9 %finish_step.1 = (bf16[256,1024]{1,0:T(8,128)(2,1)}, f32[256,1024]{1,0:T(8,128)}, f32[4,4,1024]{2,1,0:T(4,128)}, f32[1,1]{1,0:T(1,128)}, f32[4,4,1024]{2,1,0:T(4...) custom-call(f32[4,4,1024]{2,1,0:T(4,128)} %factors.3, f32[4,4,1024]{2,1,0:T(4,128)} %first_moment.1, ...), custom_call_target="tpu_custom_call" | custom-call | tf_op jit(solution)/shard_map/finish_step/pallas_call | solution.py:977
where the time goes:
time: 122 us
  Pallas kernels  121 us (99%)
    pallas_call x1, Pallas kernels, fused(): pl.pallas_call(functools.partial(fused_kernel, planes), name='block_step'...  117 us
    pallas_call x1, Pallas kernels, fused(): pl.pallas_call(finish_kernel, name='finish_step', out_shape=(rows, jax.Sh...  3.92 us

commit v1 on v0

--- a/solution.py
+++ b/solution.py
@@ -334,8 +334,8 @@
     bo_r, ig_r, summed,
     tok, n1, go, wq, wkv, wo, fcw, pw, kv, qs, p0, p1, mix, inv, attn_own, attn_s, attn_r,
     res, n2, acc_a, acc_b, gnt_s, gnt_r, gnt_xs, gnt_xr, mlp_s, mlp_r, mlp_xs, mlp_xr,
-    gr, gr_b, bo_f, bo_s, gq, dos, gno_s, gno_r, gno_xs, gno_xr, ig_s,
-    fpad, f02, f1p, f3kv, down, gd_scr, fg_a, fg_q, fg_v, ps, ps_r, plane_buf, z_buf, fin,
+    gr_b, bo_f, bo_s, gq, dos, gno_s, gno_r, gno_xs, gno_xr, ig_s,
+    f02, f1p, f3kv, down, gd_scr, fg_a, fg_q, fg_v, ps, ps_r, plane_buf, z_buf, fin,
     chain_send, chain_recv, pair_send, pair_recv, load_sem, ssem, rsem,
 ):
     d = lax.axis_index("dp")
@@ -365,6 +365,12 @@
     def other_rows(h, side):
         return at(512 * h + 256 * side + 128 * (1 - c), 128)
 
+    def ff_own(h, side):
+        return at(512 * side + 256 * h + 128 * c, 128)
+
+    def ff_other(h, side):
+        return at(512 * side + 256 * h + 128 * (1 - c), 128)
+
     def remote_to(src, dst, out_index, in_index, device):
         return pltpu.make_async_remote_copy(
             src_ref=src, dst_ref=dst, send_sem=ssem.at[out_index], recv_sem=rsem.at[in_index],
@@ -404,10 +410,19 @@
     pl.semaphore_wait(barrier, len(partners))
 
     doc = []
-    for first, source, target in ((0, tokens, tok), (4, grad_out, go)):
-        for r in range(4):
-            part = pl.ds(256 * r, 256)
-            doc.append((source.at[part, :], target.at[part, :], first + r))
+    for r in range(4):
+        part = pl.ds(256 * r, 256)
+        doc.append((tokens.at[part, :], tok.at[part, :], r))
+    place = jnp.where(c == y, 0, 512)
+    grads = [
+        (grad_out.at[rows_of(h, x), :], go.at[at(place + 256 * h, 256), :], 4 + h) for h in range(2)
+    ]
+    other_place = 512 - place
+    grads_in = [
+        (grad_out.at[rows_of(h, x), :], go.at[at(other_place + 256 * h, 256), :], 4 + h) for h in range(2)
+    ]
+    for h in range(2):
+        pltpu.make_async_copy(*grads[h][:2], load_sem.at[6 + h]).start()
 
     @pl.when(c == y)
     def _():
@@ -422,6 +437,8 @@
                 remote(*item, nbr).wait_send()
 
     pending.append(doc_sent)
+    for item in grads:
+        send(remote(*item, nbr))
 
     def doc_wait(index):
         remote(*doc[index], nbr).wait_recv()
@@ -463,7 +480,7 @@
         return pltpu.make_async_remote_copy(
             src_ref=pair_piece(step, pair, parity), dst_ref=pair_piece(1, pair, parity),
             send_sem=pair_send.at[step, pair], recv_sem=pair_recv.at[step, pair],
-            device_id=(y_nbr, zs[0])[step], device_id_type=MESH,
+            device_id=(x_nbr, zs[0])[step], device_id_type=MESH,
         )
 
     def pair_pump(pair):
@@ -478,16 +495,21 @@
         loads[matrix].wait()
         send(hop(1, 2 * matrix))
         send(hop(1, 2 * matrix + 1))
-
-    fpad[...] = jnp.zeros_like(fpad)
+    loads[4].wait()
+    loads[5].wait()
+    for pair in range(2):
+        pair_hop(0, pair, odd).start()
+
+    fpad = acc_b.at[0:128, :]
+    fpad[...] = jnp.zeros(fpad.shape, F32)
     fpad[0:4, :] = factors[0]
     fpad[4:8, :] = factors[2]
     f02[...] = fpad[...].astype(BF)
-    fpad[...] = jnp.zeros_like(fpad)
+    fpad[...] = jnp.zeros(fpad.shape, F32)
     for s in range(4):
         fpad[0:4, 128 * s : 128 * s + 128] = factors[1, :, pl.ds(column[s], 128)]
     f1p[...] = fpad[:, :512].astype(BF)
-    fpad[...] = jnp.zeros_like(fpad)
+    fpad[...] = jnp.zeros(fpad.shape, F32)
     for s in range(4):
         fpad[4:8, 256 * s + 128 : 256 * s + 256] = factors[3, :, pl.ds(column[s], 128)]
     f3kv[...] = fpad[...].astype(BF)
@@ -529,9 +551,6 @@
     row_pos = lax.broadcasted_iota(jnp.int32, (512, 512), 0) % 256 + 256 * x
     allowed = column_pos <= row_pos
 
-    loads[4].wait()
-    loads[5].wait()
-
     @pl.loop(0, 4)
     def _(s):
         @pl.when(s == 1)
@@ -547,7 +566,7 @@
         @pl.when(s == 3)
         def _():
             pump(7, False)
-            for pair in range(PAIRS):
+            for pair in range(2, PAIRS):
                 pair_hop(0, pair, odd).start()
 
         both_lanes, lanes = at(256 * s, 256), at(128 * s, 128)
@@ -592,6 +611,7 @@
     attn_s[...] = heads_out(1 - c).astype(BF)
     to_nbr = send(remote(attn_s, attn_r, 8, nbr))
     attn_own[...] = heads_out(c)
+    pair_pump(0)
     to_nbr.wait_recv()
 
     gathered = []
@@ -601,21 +621,24 @@
         residual = tok[rows, :].astype(F32) + attn_own[part, :] + attn_r[part, :].astype(F32)
         res[part, :] = residual
         unit, _ = unit_of(residual)
+        rows = ff_own(h, 0)
         n2[rows, :] = (unit * gain_two + bias_two).astype(BF)
-        gathered.append(send(remote(n2.at[rows, :], n2.at[rows, :], 11 + h, x_nbr)))
+        gathered.append(send(remote(n2.at[rows, :], n2.at[ff_own(h, 1), :], 11 + h, y_nbr)))
         gathered.append(send(remote(n2.at[rows, :], n2.at[rows, :], 9 + h, nbr)))
-    for r in range(4):
-        doc_wait(4 + r)
+    pair_pump(1)
+    for h in range(2):
+        pltpu.make_async_copy(*grads[h][:2], load_sem.at[6 + h]).wait()
+        remote(*grads_in[h], nbr).wait_recv()
     gathered[1].wait_recv()
     gathered[3].wait_recv()
 
     def pass_on(h):
         gathered[2 * h].wait_recv()
-        rows = own_rows(h, 1 - x)
+        rows = ff_own(h, 1)
         remote(n2.at[rows, :], n2.at[rows, :], 13 + h, nbr).start()
 
     def passed_on(h):
-        rows = own_rows(h, 1 - x)
+        rows = ff_own(h, 1)
         return remote(n2.at[rows, :], n2.at[rows, :], 13 + h, nbr)
 
     def sum_copy(source, target, first, h, j):
@@ -623,44 +646,45 @@
         return remote(source.at[h, part, :], target.at[h, part, :], first + 2 * h + j, nbr)
 
     def to_core(acc, source, target, first, h):
-        for j, side in enumerate((1 - x, x)):
-            source[h, 128 * j : 128 * j + 128, :] = acc[other_rows(h, side), :].astype(BF)
+        for j, side in enumerate((1, 0)):
+            source[h, 128 * j : 128 * j + 128, :] = acc[ff_other(h, side), :].astype(BF)
             sum_copy(source, target, first, h, j).start()
 
     def to_side(acc, source, target, out, out_target, first, side_first, h):
         sum_copy(source, target, first, h, 0).wait_recv()
-        out[h] = (acc[own_rows(h, 1 - x), :] + target[h, 0:128, :].astype(F32)).astype(BF)
-        return send(remote(out.at[h], out_target.at[h], side_first + h, x_nbr))
+        out[h] = (acc[ff_own(h, 1), :] + target[h, 0:128, :].astype(F32)).astype(BF)
+        return send(remote(out.at[h], out_target.at[h], side_first + h, y_nbr))
 
     @pl.loop(0, 8)
     def _(unit):
-        @pl.when(unit == 0)
-        def _():
-            pair_pump(0)
+        @pl.when(unit == 1)
+        def _():
+            pair_pump(2)
 
         @pl.when(unit == 2)
         def _():
-            for pair in (1, 2):
-                pair_pump(pair)
+            pair_pump(3)
             pass_on(0)
-            for pair in (3, 4):
-                pair_pump(pair)
+            pair_pump(4)
             pair_wait(range(0, 4))
 
         @pl.when(unit == 3)
         def _():
+            pair_pump(5)
             pass_on(1)
-            pair_pump(5)
             for h in range(2):
                 passed_on(h).wait_recv()
 
+        @pl.when(unit == 4)
+        def _():
+            pair_pump(6)
+
         @pl.when(unit == 5)
         def _():
-            pair_pump(6)
+            pair_pump(7)
 
         @pl.when(unit == 6)
         def _():
-            pair_pump(7)
             pair_wait(range(4, 8))
 
         @pl.when(unit == 7)
@@ -670,10 +694,10 @@
         flag = lambda value: jnp.where(value, 1, 0)
         slot = flag(jnp.logical_or(unit == 2, unit >= 5))
         part = flag(jnp.logical_or(unit >= 6, jnp.logical_or(unit == 1, unit == 4)))
-        side = jnp.where(unit < 3, x, 1 - x)
+        side = flag(unit >= 3)
         last_half = 7 - unit
         starts = [
-            jnp.where(unit < 6, 512 * h + 256 * side, 512 * last_half + 256 * h) for h in range(2)
+            jnp.where(unit < 6, 512 * side + 256 * h, 512 * h + 256 * last_half) for h in range(2)
         ]
         tiles = [at(start, 256) for start in starts]
         lanes = at(256 * part, 256)
@@ -708,16 +732,18 @@
     for h in range(2):
         part = slice(128 * h, 128 * h + 128)
         sum_copy(mlp_s, mlp_r, 44, h, 1).wait_recv()
-        bo_f[part, :] = res[part, :] + acc_a[own_rows(h, x), :] + mlp_r[h, 128:256, :].astype(F32)
+        bo_f[part, :] = res[part, :] + acc_a[ff_own(h, 0), :] + mlp_r[h, 128:256, :].astype(F32)
+
+    gr = attn_own
 
     def residual_back(h):
         part = slice(128 * h, 128 * h + 128)
         unit, inverse = unit_of(res[part, :])
         sum_copy(gnt_s, gnt_r, 40, h, 1).wait_recv()
-        total = acc_b[own_rows(h, x), :] + gnt_r[h, 128:256, :].astype(F32)
+        total = acc_b[ff_own(h, 0), :] + gnt_r[h, 128:256, :].astype(F32)
         gnt_side[h].wait_recv()
         scaled = (total + gnt_xr[h].astype(F32)) * gain_two
-        grad = go[own_rows(h, x), :].astype(F32) + unit_back(scaled, unit, inverse)
+        grad = go[ff_own(h, 0), :].astype(F32) + unit_back(scaled, unit, inverse)
         gr[part, :] = grad
         local = at(256 * h + 128 * c, 128)
         gr_b[local, :] = grad.astype(BF)
@@ -776,16 +802,16 @@
         part = pl.ds(128 * j, 128)
         return remote(gno_s.at[h, part, :], gno_r.at[h, part, :], 27 + 2 * h + j, nbr)
 
-    def rows_back(h):
-        for j, side in enumerate((1 - x, x)):
-            rows = rows_of(h, side)
-            grad = mm_nt(acc_a[rows, :].astype(BF), wkv[...])
-            grad += mm(gd_scr[at(256 * side, 256), :].astype(BF), f02[...])
-            if j:
-                grad += mm_nt(gq[...], wq[...])
-            acc_b[rows, :] = grad
-            gno_s[h, 128 * j : 128 * j + 128, :] = acc_b[other_rows(h, side), :].astype(BF)
-            send(rows_copy(h, j))
+    def rows_back(h, j):
+        side = x if j else 1 - x
+        rows = rows_of(h, side)
+        grad = mm_nt(acc_a[rows, :].astype(BF), wkv[...])
+        grad += mm(gd_scr[at(256 * side, 256), :].astype(BF), f02[...])
+        if j:
+            grad += mm_nt(gq[...], wq[...])
+        acc_b[rows, :] = grad
+        gno_s[h, 128 * j : 128 * j + 128, :] = acc_b[other_rows(h, side), :].astype(BF)
+        send(rows_copy(h, j))
 
     side_copies = {}
 
@@ -833,17 +859,13 @@
 
     to_nbr = residual_back(0)
     factors_back(1)
-    rows_back(1)
+    rows_back(1, 0)
+    rows_back(1, 1)
     to_nbr.wait_recv()
     mixture_back(0)
     reduce_rows(1)
     scores_back(0, 0, 4)
 
-    for h in (1, 0):
-        part = slice(128 * h, 128 * h + 128)
-        mlp_side[h].wait_recv()
-        bo_s[part, :] = (bo_f[part, :] + mlp_xr[h].astype(F32)).astype(BF)
-        to_owner(bo_s.at[part, :], bo_r.at[at(128 * c, 128), :], h, 60 + h, 62)
     factors_back(0)
 
     ps[0:8, :] = fg_a[...]
@@ -853,7 +875,7 @@
             down_rows, fg_q[:, 128 * s : 128 * s + 128], fg_v[:, 256 * s + 128 : 256 * s + 256]
         )
     core_sum = send(remote(ps, ps_r, 33, nbr))
-    rows_back(0)
+    rows_back(0, 0)
     core_sum.wait_recv()
     eight = at(8 * c, 8)
     plane_buf[t] = ps[eight, :] + ps_r[eight, :]
@@ -861,6 +883,12 @@
         send(remote(plane_buf.at[t], plane_buf.at[t], 35 + k, device)) for k, device in enumerate(plane)
     ]
     reduce_rows(0)
+    for h in (1, 0):
+        part = slice(128 * h, 128 * h + 128)
+        mlp_side[h].wait_recv()
+        bo_s[part, :] = (bo_f[part, :] + mlp_xr[h].astype(F32)).astype(BF)
+        to_owner(bo_s.at[part, :], bo_r.at[at(128 * c, 128), :], h, 60 + h, 62)
+    rows_back(0, 1)
     for k in range(2):
         input_rows(1, k)
     for copy in copies:
@@ -953,12 +981,12 @@
         buf(4, 512, 1024), acc(512, 512), acc(2, 512, 512), acc(256, 1024), *quarter,
         acc(256, 1024), buf(1024, 1024), acc(1024, 1024), acc(1024, 1024),
         *halves, *eighths, *halves, *eighths,
-        acc(256, 1024), buf(512, 1024), acc(256, 1024), buf(256, 1024), buf(256, 512), buf(2, 512, 512),
+        buf(512, 1024), acc(256, 1024), buf(256, 1024), buf(256, 512), buf(2, 512, 512),
         *halves, *eighths, buf(256, 1024),
-        acc(128, 1024), buf(128, 1024), buf(128, 512), buf(128, 1024), buf(1024, 128), acc(512, 128),
+        buf(128, 1024), buf(128, 512), buf(128, 1024), buf(1024, 128), acc(512, 128),
         acc(8, 1024), acc(8, 512), acc(8, 1024), acc(16, 1024), acc(16, 1024), acc(4, 8, 1024),
         acc(2 * planes, 8, 1024), acc(16, 1024),
-        sems(3, GROUPS), sems(3, GROUPS), sems(2, PAIRS), sems(2, PAIRS), sems(6), sems(64 + planes),
+        sems(3, GROUPS), sems(3, GROUPS), sems(2, PAIRS), sems(2, PAIRS), sems(8), sems(64 + planes),
         sems(64 + planes),
     ]
     rows = jax.ShapeDtypeStruct((256, 1024), BF)

time: 122 us -> 115 us (0.943)
  Pallas kernels: 121 us -> 114 us
    pallas_call x1, Pallas kernels: 117 us -> 110 us  [fused(): pl.pallas_call(functools.partial(fused_kernel, planes), name='block_step'...]
where the time goes in v1:
time: 115 us
  Pallas kernels  114 us (99%)
    pallas_call x1, Pallas kernels, fused(): pl.pallas_call(functools.partial(fused_kernel, planes), name='block_step'...  110 us
    pallas_call x1, Pallas kernels, fused(): pl.pallas_call(finish_kernel, name='finish_step', out_shape=(rows, jax.Sh...  3.92 us

profile of v1, /device:TPU:1, one launch (start us, length us, event | category | flops | bytes accessed | tf_op | source)
XLA Modules:
  0.0 114.7 jit_solution(5660098141087110071)
XLA Ops:
  0.6 109.9 %block_step.1 = (bf16[256,1024]{1,0:T(8,128)(2,1)}, bf16[256,1024]{1,0:T(8,128)(2,1)}, f32[16,1024]{1,0:T(8,128)}) custom-call(bf16[1024,1024]{1,0:T(8,128)(2,1)} %tokens.1, f32[4,1024]{1,0:T(4,128)} %norm_params.1, bf16[3,1024,256]{2,1,0:T(8,128)(2,1)} %wqkv.1, bf16[256,1024]{1,0:T(8,128)(2,1)} %w_out.1, bf16[1024,1024]{1,0:T(8,128)(2,1)} %w_fc.1, ...), custom_call_target="tpu_custom_call" | custom-call | tf_op jit(solution)/shard_map/block_step/pallas_call | solution.py:993
  110.6 3.9 %finish_step.1 = (bf16[256,1024]{1,0:T(8,128)(2,1)}, f32[256,1024]{1,0:T(8,128)}, f32[4,4,1024]{2,1,0:T(4,128)}, f32[1,1]{1,0:T(1,128)}, f32[4,4,1024]{2,1,0:T(4...) custom-call(f32[4,4,1024]{2,1,0:T(4,128)} %factors.3, f32[4,4,1024]{2,1,0:T(4,128)} %first_moment.1, ...), custom_call_target="tpu_custom_call" | custom-call | tf_op jit(solution)/shard_map/finish_step/pallas_call | solution.py:1005

commit v2 on v1

--- a/solution.py
+++ b/solution.py
@@ -602,6 +602,7 @@
         pending.append(hop(3, group).wait_send)
     for pair in range(PAIRS):
         pending.append(pair_hop(0, pair, odd).wait_send)
+    pair_pump(0)
     passed(range(6, 8))
 
     def heads_out(sub):
@@ -610,8 +611,9 @@
 
     attn_s[...] = heads_out(1 - c).astype(BF)
     to_nbr = send(remote(attn_s, attn_r, 8, nbr))
+    pair_pump(1)
     attn_own[...] = heads_out(c)
-    pair_pump(0)
+    pair_pump(2)
     to_nbr.wait_recv()
 
     gathered = []
@@ -625,7 +627,7 @@
         n2[rows, :] = (unit * gain_two + bias_two).astype(BF)
         gathered.append(send(remote(n2.at[rows, :], n2.at[ff_own(h, 1), :], 11 + h, y_nbr)))
         gathered.append(send(remote(n2.at[rows, :], n2.at[rows, :], 9 + h, nbr)))
-    pair_pump(1)
+    pair_pump(3)
     for h in range(2):
         pltpu.make_async_copy(*grads[h][:2], load_sem.at[6 + h]).wait()
         remote(*grads_in[h], nbr).wait_recv()
@@ -659,29 +661,21 @@
     def _(unit):
         @pl.when(unit == 1)
         def _():
-            pair_pump(2)
+            pair_pump(4)
 
         @pl.when(unit == 2)
         def _():
-            pair_pump(3)
+            pair_wait(range(0, 4))
             pass_on(0)
-            pair_pump(4)
-            pair_wait(range(0, 4))
+            pair_pump(5)
 
         @pl.when(unit == 3)
         def _():
-            pair_pump(5)
+            pair_pump(6)
             pass_on(1)
+            pair_pump(7)
             for h in range(2):
                 passed_on(h).wait_recv()
-
-        @pl.when(unit == 4)
-        def _():
-            pair_pump(6)
-
-        @pl.when(unit == 5)
-        def _():
-            pair_pump(7)
 
         @pl.when(unit == 6)
         def _():

time: 115 us -> 111 us (0.965)
  Pallas kernels: 114 us -> 110 us
    pallas_call x1, Pallas kernels: 110 us -> 106 us  [fused(): pl.pallas_call(functools.partial(fused_kernel, planes), name='block_step'...]
where the time goes in v2:
time: 111 us
  Pallas kernels  110 us (99%)
    pallas_call x1, Pallas kernels, fused(): pl.pallas_call(functools.partial(fused_kernel, planes), name='block_step'...  106 us
    pallas_call x1, Pallas kernels, fused(): pl.pallas_call(finish_kernel, name='finish_step', out_shape=(rows, jax.Sh...  3.92 us

profile of v2, /device:TPU:1, one launch (start us, length us, event | category | flops | bytes accessed | tf_op | source)
XLA Modules:
  0.0 110.9 jit_solution(7015766815757955942)
XLA Ops:
  0.6 106.2 %block_step.1 = (bf16[256,1024]{1,0:T(8,128)(2,1)}, bf16[256,1024]{1,0:T(8,128)(2,1)}, f32[16,1024]{1,0:T(8,128)}) custom-call(bf16[1024,1024]{1,0:T(8,128)(2,1)} %tokens.1, f32[4,1024]{1,0:T(4,128)} %norm_params.1, bf16[3,1024,256]{2,1,0:T(8,128)(2,1)} %wqkv.1, bf16[256,1024]{1,0:T(8,128)(2,1)} %w_out.1, bf16[1024,1024]{1,0:T(8,128)(2,1)} %w_fc.1, ...), custom_call_target="tpu_custom_call" | custom-call | tf_op jit(solution)/shard_map/block_step/pallas_call | solution.py:987
  106.8 3.9 %finish_step.1 = (bf16[256,1024]{1,0:T(8,128)(2,1)}, f32[256,1024]{1,0:T(8,128)}, f32[4,4,1024]{2,1,0:T(4,128)}, f32[1,1]{1,0:T(1,128)}, f32[4,4,1024]{2,1,0:T(4...) custom-call(f32[4,4,1024]{2,1,0:T(4,128)} %factors.3, f32[4,4,1024]{2,1,0:T(4,128)} %first_moment.1, ...), custom_call_target="tpu_custom_call" | custom-call | tf_op jit(solution)/shard_map/finish_step/pallas_call | solution.py:999

commit v3 on v2

--- a/solution.py
+++ b/solution.py
@@ -407,6 +407,22 @@
     partners = [nbr, x_nbr, y_nbr] + zs
     for device in partners:
         pl.semaphore_signal(barrier, inc=1, device_id=device, device_id_type=MESH)
+    fpad = acc_b.at[0:128, :]
+    fpad[...] = jnp.zeros(fpad.shape, F32)
+    fpad[0:4, :] = factors[0]
+    fpad[4:8, :] = factors[2]
+    f02[...] = fpad[...].astype(BF)
+    fpad[...] = jnp.zeros(fpad.shape, F32)
+    for s in range(4):
+        fpad[0:4, 128 * s : 128 * s + 128] = factors[1, :, pl.ds(column[s], 128)]
+    f1p[...] = fpad[:, :512].astype(BF)
+    fpad[...] = jnp.zeros(fpad.shape, F32)
+    for s in range(4):
+        fpad[4:8, 256 * s + 128 : 256 * s + 256] = factors[3, :, pl.ds(column[s], 128)]
+    f3kv[...] = fpad[...].astype(BF)
+    ps[...] = jnp.zeros_like(ps)
+    acc_a[...] = jnp.zeros_like(acc_a)
+    acc_b[...] = jnp.zeros_like(acc_b)
     pl.semaphore_wait(barrier, len(partners))
 
     doc = []
@@ -500,21 +516,6 @@
     for pair in range(2):
         pair_hop(0, pair, odd).start()
 
-    fpad = acc_b.at[0:128, :]
-    fpad[...] = jnp.zeros(fpad.shape, F32)
-    fpad[0:4, :] = factors[0]
-    fpad[4:8, :] = factors[2]
-    f02[...] = fpad[...].astype(BF)
-    fpad[...] = jnp.zeros(fpad.shape, F32)
-    for s in range(4):
-        fpad[0:4, 128 * s : 128 * s + 128] = factors[1, :, pl.ds(column[s], 128)]
-    f1p[...] = fpad[:, :512].astype(BF)
-    fpad[...] = jnp.zeros(fpad.shape, F32)
-    for s in range(4):
-        fpad[4:8, 256 * s + 128 : 256 * s + 256] = factors[3, :, pl.ds(column[s], 128)]
-    f3kv[...] = fpad[...].astype(BF)
-    ps[...] = jnp.zeros_like(ps)
-
     gain_one, bias_one = norm_params[0:1, :], norm_params[1:2, :]
     gain_two, bias_two = norm_params[2:3, :], norm_params[3:4, :]
     def first_norm(r):
@@ -538,8 +539,6 @@
         down[rows, :] = mm_nt(n1[rows, :], f02[...]).astype(BF)
 
     pump(1)
-    acc_a[...] = jnp.zeros_like(acc_a)
-    acc_b[...] = jnp.zeros_like(acc_b)
     first_head = lax.broadcasted_iota(jnp.int32, (256, 512), 1) % 128 < 64
     first_lanes = first_head[:, 0:128]
 
@@ -715,18 +714,25 @@
             pending.append(sum_copy(gnt_s, gnt_r, 40, h, j).wait_send)
             pending.append(sum_copy(mlp_s, mlp_r, 44, h, j).wait_send)
 
-    gnt_side, mlp_side = [None, None], [None, None]
+    gnt_side = [None, None]
+    gnt_side[1] = to_side(acc_b, gnt_s, gnt_r, gnt_xs, gnt_xr, 40, 17, 1)
     to_core(acc_b, gnt_s, gnt_r, 40, 0)
-    for h in (1, 0):
-        gnt_side[h] = to_side(acc_b, gnt_s, gnt_r, gnt_xs, gnt_xr, 40, 17, h)
+    gnt_side[0] = to_side(acc_b, gnt_s, gnt_r, gnt_xs, gnt_xr, 40, 17, 0)
     for h in (1, 0):
         to_core(acc_a, mlp_s, mlp_r, 44, h)
+    near, far = y, 1 - y
     for h in (1, 0):
-        mlp_side[h] = to_side(acc_a, mlp_s, mlp_r, mlp_xs, mlp_xr, 44, 21, h)
-    for h in range(2):
-        part = slice(128 * h, 128 * h + 128)
-        sum_copy(mlp_s, mlp_r, 44, h, 1).wait_recv()
-        bo_f[part, :] = res[part, :] + acc_a[ff_own(h, 0), :] + mlp_r[h, 128:256, :].astype(F32)
+        for j in range(2):
+            sum_copy(mlp_s, mlp_r, 44, h, j).wait_recv()
+
+    def chip_sum(h, side):
+        return acc_a[ff_own(h, side), :] + mlp_r[h, 128 * (1 - side) : 128 * (1 - side) + 128, :].astype(F32)
+
+    mlp_xs[0] = chip_sum(far, 1).astype(BF)
+    mlp_xs[1] = (res[at(128 * far, 128), :] + chip_sum(far, 0)).astype(BF)
+    mlp_side = [send(remote(mlp_xs.at[k], mlp_xr.at[k], 21 + k, y_nbr)) for k in range(2)]
+    bo_f[0] = res[at(128 * near, 128), :] + chip_sum(near, 0)
+    bo_f[1] = chip_sum(near, 1)
 
     gr = attn_own
 
@@ -847,9 +853,8 @@
         ig_s[out, :] = (gr[out, :] + unit_back(scaled, unit, inverse)).astype(BF)
         to_owner(ig_s.at[out, :], ig_r.at[at(128 * c + 64 * k, 64), :], h, 52 + 2 * h + k, 56 + 2 * k)
 
-    @pl.loop(0, 2)
-    def _(group):
-        scores_back(1, 2 * group, 2)
+    scores_back(1, 0, 2)
+    scores_back(1, 2, 2)
 
     to_nbr = residual_back(0)
     factors_back(1)
@@ -877,11 +882,14 @@
         send(remote(plane_buf.at[t], plane_buf.at[t], 35 + k, device)) for k, device in enumerate(plane)
     ]
     reduce_rows(0)
-    for h in (1, 0):
-        part = slice(128 * h, 128 * h + 128)
-        mlp_side[h].wait_recv()
-        bo_s[part, :] = (bo_f[part, :] + mlp_xr[h].astype(F32)).astype(BF)
-        to_owner(bo_s.at[part, :], bo_r.at[at(128 * c, 128), :], h, 60 + h, 62)
+    for k in range(2):
+        mlp_side[k].wait_recv()
+        bo_s[k] = (bo_f[k] + mlp_xr[k].astype(F32)).astype(BF)
+    kept = jnp.where(c == y, 0, 1)
+    home = pl.ds(pl.multiple_of(128 * c, 128), 128)
+    bo_home = pltpu.make_async_copy(bo_s.at[kept], bo_r.at[home, :], load_sem.at[1])
+    bo_home.start()
+    bo_away = send(remote(bo_s.at[1 - kept], bo_r.at[home, :], 60, nbr))
     rows_back(0, 1)
     for k in range(2):
         input_rows(1, k)
@@ -907,9 +915,9 @@
     result = pltpu.make_async_copy(fin, summed, load_sem.at[0])
     result.start()
 
+    bo_home.wait()
+    bo_away.wait_recv()
     for core in range(2):
-        part = pl.ds(128 * core, 128)
-        remote_to(bo_s.at[pl.ds(0, 128), :], bo_r.at[part, :], 60, 62 + core, nbr).wait_recv()
         for k in range(2):
             part = pl.ds(128 * core + 64 * k, 64)
             remote_to(ig_s.at[pl.ds(0, 64), :], ig_r.at[part, :], 52, 56 + 2 * k + core, nbr).wait_recv()
@@ -975,7 +983,7 @@
         buf(4, 512, 1024), acc(512, 512), acc(2, 512, 512), acc(256, 1024), *quarter,
         acc(256, 1024), buf(1024, 1024), acc(1024, 1024), acc(1024, 1024),
         *halves, *eighths, *halves, *eighths,
-        buf(512, 1024), acc(256, 1024), buf(256, 1024), buf(256, 512), buf(2, 512, 512),
+        buf(512, 1024), acc(2, 128, 1024), buf(2, 128, 1024), buf(256, 512), buf(2, 512, 512),
         *halves, *eighths, buf(256, 1024),
         buf(128, 1024), buf(128, 512), buf(128, 1024), buf(1024, 128), acc(512, 128),
         acc(8, 1024), acc(8, 512), acc(8, 1024), acc(16, 1024), acc(16, 1024), acc(4, 8, 1024),

time: 111 us -> 109 us (0.982)
  Pallas kernels: 110 us -> 108 us
    pallas_call x1, Pallas kernels: 106 us -> 104 us  [fused(): pl.pallas_call(functools.partial(fused_kernel, planes), name='block_step'...]
where the time goes in v3:
time: 109 us
  Pallas kernels  108 us (99%)
    pallas_call x1, Pallas kernels, fused(): pl.pallas_call(functools.partial(fused_kernel, planes), name='block_step'...  104 us
    pallas_call x1, Pallas kernels, fused(): pl.pallas_call(finish_kernel, name='finish_step', out_shape=(rows, jax.Sh...  3.92 us

profile of v3, /device:TPU:1, one launch (start us, length us, event | category | flops | bytes accessed | tf_op | source)
XLA Modules:
  0.0 109.1 jit_solution(7959972421581028935)
XLA Ops:
  0.6 104.3 %block_step.1 = (bf16[256,1024]{1,0:T(8,128)(2,1)}, bf16[256,1024]{1,0:T(8,128)(2,1)}, f32[16,1024]{1,0:T(8,128)}) custom-call(bf16[1024,1024]{1,0:T(8,128)(2,1)} %tokens.1, f32[4,1024]{1,0:T(4,128)} %norm_params.1, bf16[3,1024,256]{2,1,0:T(8,128)(2,1)} %wqkv.1, bf16[256,1024]{1,0:T(8,128)(2,1)} %w_out.1, bf16[1024,1024]{1,0:T(8,128)(2,1)} %w_fc.1, ...), custom_call_target="tpu_custom_call" | custom-call | tf_op jit(solution)/shard_map/block_step/pallas_call | solution.py:995
  105.0 3.9 %finish_step.1 = (bf16[256,1024]{1,0:T(8,128)(2,1)}, f32[256,1024]{1,0:T(8,128)}, f32[4,4,1024]{2,1,0:T(4,128)}, f32[1,1]{1,0:T(1,128)}, f32[4,4,1024]{2,1,0:T(4...) custom-call(f32[4,4,1024]{2,1,0:T(4,128)} %factors.3, f32[4,4,1024]{2,1,0:T(4,128)} %first_moment.1, ...), custom_call_target="tpu_custom_call" | custom-call | tf_op jit(solution)/shard_map/finish_step/pallas_call | solution.py:1007

commit v4 on v3

--- a/solution.py
+++ b/solution.py
@@ -665,16 +665,19 @@
         @pl.when(unit == 2)
         def _():
             pair_wait(range(0, 4))
+            pair_pump(5)
+
+        @pl.when(unit == 3)
+        def _():
             pass_on(0)
-            pair_pump(5)
-
-        @pl.when(unit == 3)
-        def _():
             pair_pump(6)
+            passed_on(0).wait_recv()
+
+        @pl.when(unit == 4)
+        def _():
+            pair_pump(7)
             pass_on(1)
-            pair_pump(7)
-            for h in range(2):
-                passed_on(h).wait_recv()
+            passed_on(1).wait_recv()
 
         @pl.when(unit == 6)
         def _():
@@ -685,26 +688,26 @@
             to_core(acc_b, gnt_s, gnt_r, 40, 1)
 
         flag = lambda value: jnp.where(value, 1, 0)
+        single = jnp.logical_or(unit == 3, unit == 4)
         slot = flag(jnp.logical_or(unit == 2, unit >= 5))
-        part = flag(jnp.logical_or(unit >= 6, jnp.logical_or(unit == 1, unit == 4)))
-        side = flag(unit >= 3)
-        last_half = 7 - unit
-        starts = [
-            jnp.where(unit < 6, 512 * side + 256 * h, 512 * h + 256 * last_half) for h in range(2)
-        ]
-        tiles = [at(start, 256) for start in starts]
-        lanes = at(256 * part, 256)
-        pre = [mm(n2[rows, :], fcw[slot, :, lanes]) for rows in tiles]
-        grad_act = [mm_nt(go[rows, :], pw[slot, lanes, :]) for rows in tiles]
-        for rows, hidden, grad in zip(tiles, pre, grad_act):
+        tiles, lanes = [], []
+        for k in range(2):
+            half = jnp.where(single, unit - 3, jnp.where(unit >= 6, 7 - unit, k))
+            side = jnp.where(unit >= 6, 1 - k, flag(unit >= 3))
+            part = jnp.where(single, k, flag(jnp.logical_or(unit >= 6, unit == 1)))
+            tiles.append(at(512 * side + 256 * half, 256))
+            lanes.append(at(256 * part, 256))
+        pre = [mm(n2[rows, :], fcw[slot, :, lane]) for rows, lane in zip(tiles, lanes)]
+        grad_act = [mm_nt(go[rows, :], pw[slot, lane, :]) for rows, lane in zip(tiles, lanes)]
+        for rows, lane, hidden, grad in zip(tiles, lanes, pre, grad_act):
             square = hidden * hidden
             tanh = jnp.tanh(GELU_SCALE * hidden * (1.0 + GELU_CUBE * square))
             half_up = 0.5 * (1.0 + tanh)
             slope = half_up + (0.5 * GELU_SCALE) * hidden * (1.0 - tanh * tanh) * (
                 1.0 + 3.0 * GELU_CUBE * square
             )
-            acc_b[rows, :] += mm_nt((grad * slope).astype(BF), fcw[slot, :, lanes])
-            acc_a[rows, :] += mm((hidden * half_up).astype(BF), pw[slot, lanes, :])
+            acc_b[rows, :] += mm_nt((grad * slope).astype(BF), fcw[slot, :, lane])
+            acc_a[rows, :] += mm((hidden * half_up).astype(BF), pw[slot, lane, :])
 
     for pair in range(PAIRS):
         pending.append(pair_hop(1, pair, odd).wait_send)
@@ -891,8 +894,6 @@
     bo_home.start()
     bo_away = send(remote(bo_s.at[1 - kept], bo_r.at[home, :], 60, nbr))
     rows_back(0, 1)
-    for k in range(2):
-        input_rows(1, k)
     for copy in copies:
         copy.wait_recv()
     z_buf[0] = plane_buf[0] + plane_buf[1] + plane_buf[2] + plane_buf[3]
@@ -902,6 +903,9 @@
 
     for k in range(len(zs)):
         send(z_copy(k))
+        if k == 0:
+            input_rows(1, 0)
+            input_rows(1, 1)
         if k < 2:
             input_rows(0, k)
         z_copy(k).wait_recv()

time: 109 us -> 109 us (level)
  no operation moved by 1% of the time
where the time goes in v4:
time: 109 us
  Pallas kernels  108 us (99%)
    pallas_call x1, Pallas kernels, fused(): pl.pallas_call(functools.partial(fused_kernel, planes), name='block_step'...  104 us
    pallas_call x1, Pallas kernels, fused(): pl.pallas_call(finish_kernel, name='finish_step', out_shape=(rows, jax.Sh...  3.92 us

profile of v4, /device:TPU:1, one launch (start us, length us, event | category | flops | bytes accessed | tf_op | source)
XLA Modules:
  0.0 109.1 jit_solution(12458204094734448482)
XLA Ops:
  0.6 104.4 %block_step.1 = (bf16[256,1024]{1,0:T(8,128)(2,1)}, bf16[256,1024]{1,0:T(8,128)(2,1)}, f32[16,1024]{1,0:T(8,128)}) custom-call(bf16[1024,1024]{1,0:T(8,128)(2,1)} %tokens.1, f32[4,1024]{1,0:T(4,128)} %norm_params.1, bf16[3,1024,256]{2,1,0:T(8,128)(2,1)} %wqkv.1, bf16[256,1024]{1,0:T(8,128)(2,1)} %w_out.1, bf16[1024,1024]{1,0:T(8,128)(2,1)} %w_fc.1, ...), custom_call_target="tpu_custom_call" | custom-call | tf_op jit(solution)/shard_map/block_step/pallas_call | solution.py:999
  105.0 3.9 %finish_step.1 = (bf16[256,1024]{1,0:T(8,128)(2,1)}, f32[256,1024]{1,0:T(8,128)}, f32[4,4,1024]{2,1,0:T(4,128)}, f32[1,1]{1,0:T(1,128)}, f32[4,4,1024]{2,1,0:T(4...) custom-call(f32[4,4,1024]{2,1,0:T(4,128)} %factors.3, f32[4,4,1024]{2,1,0:T(4,128)} %first_moment.1, ...), custom_call_target="tpu_custom_call" | custom-call | tf_op jit(solution)/shard_map/finish_step/pallas_call | solution.py:1011
